TPU v7x, 256 devices: a whole 4x4x8 slice. The times are simulated.
256 devices in a mesh: bx: 16 (over y, x), by: 16 (over z, core).
Axes of the slice: x: 4, y: 4, z: 8, core: 2. Of those that a mesh axis runs over, the one named last changes fastest.
Arguments:
- coefficients: float32 [16, 16, 2, 64, 2048], P('bx', 'by'), may hold values from -1.5 to 1.5
Outputs:
- transformed: float32 [16, 16, 2, 64, 2048], P('bx', 'by')
All inputs are finite; a program needn't handle non-finite values.
Results may differ from a plain program's by a relative error of at most 0.0006.
Values sent between devices are 32-bit elements; how exact they have to be, the bound alone decides.
A program may use at most 64 MiB of HBM per device.

v0:
```python
import math

import jax
import jax.numpy as jnp
from jax import lax
from jax.sharding import PartitionSpec as P

TWO_PI = 2.0 * math.pi


def swapped(array, axis, bit):
    return lax.ppermute(array, axis, [(i, i ^ 1 << bit) for i in range(lax.axis_size(axis))])


def cheb_points():
    order_index = jnp.arange(4, dtype=jnp.int32).astype(jnp.float32)
    return 0.5 * jnp.cos((2.0 * order_index + 1.0) * (math.pi / 8.0))


def child_weights(child_bit):
    nodes_all = cheb_points()
    targets = (child_bit - 0.5) * 0.5 + 0.5 * nodes_all
    identity = jnp.eye(4, dtype=jnp.float32)
    numer = targets[None, None, :] - nodes_all[None, :, None]
    denom = nodes_all[:, None, None] - nodes_all[None, :, None] + identity[:, :, None]
    factor = jnp.where(identity[:, :, None] > 0.5, jnp.ones_like(numer), numer / denom)
    return jnp.prod(factor, axis=1)


def side_weights(bit_value):
    return jnp.where(bit_value == 1, child_weights(1), child_weights(0))


def cube_matrix(bit_first, bit_second, bit_third):
    joined = jnp.einsum(
        "ad,be,cf->abcdef",
        side_weights(bit_first),
        side_weights(bit_second),
        side_weights(bit_third),
        precision=lax.Precision.HIGHEST,
        preferred_element_type=jnp.float32,
    )
    return joined.reshape(64, 64)


def bit_at(value, level_index):
    return value // 2**level_index % 2


def partner(value, level_index):
    return value + (1 - 2 * bit_at(value, level_index)) * 2**level_index


def logical_index(value, count):
    quarter = count // 4
    upper = value // quarter
    return 4 * (value % quarter) + 2 * (upper % 2) + upper // 2


def low_bits(value, level_index):
    if level_index == 0:
        return 0
    return value % 2


def phase_angle(x_first, x_second, x_third, p_first, p_second, p_third):
    radius = jnp.sqrt(p_first * p_first + p_second * p_second + p_third * p_third)
    speed = 0.05 * (
        1.0
        + 0.5 * jnp.sin(TWO_PI * x_first) * jnp.sin(TWO_PI * x_second)
        + 0.3 * jnp.cos(TWO_PI * x_third)
    )
    return TWO_PI * (x_first * p_first + x_second * p_second + x_third * p_third + speed * radius)


def centers(target_row, target_col, level_index, spatial, n_by):
    zc_count = 2**level_index
    cell_size = 0.5 ** (4 + level_index)
    group = target_row // 4 * (n_by // 4) + target_col // 4
    parent = group * spatial + jnp.arange(spatial, dtype=jnp.int32)
    cell_x = 2 * (parent // 64 * zc_count + low_bits(target_row, level_index)) + bit_at(
        target_row, level_index
    )
    cell_y = 2 * (parent // 8 % 8 * zc_count + low_bits(target_col, level_index)) + bit_at(
        target_col, level_index
    )
    cell_z = 2 * (parent[:, None] % 8 * zc_count + jnp.arange(zc_count, dtype=jnp.int32)[None, :])
    cell_z = cell_z[:, :, None] + jnp.arange(2, dtype=jnp.int32)[None, None, :]
    first = ((cell_x.astype(jnp.float32) + 0.5) * cell_size).reshape(1, spatial, 1, 1, 1, 1, 1)
    second = ((cell_y.astype(jnp.float32) + 0.5) * cell_size).reshape(1, spatial, 1, 1, 1, 1, 1)
    third = ((cell_z.astype(jnp.float32) + 0.5) * cell_size).reshape(
        1, spatial, 1, 1, zc_count, 2, 1
    )
    return (first, second, third)


def point_nodes():
    nodes_all = cheb_points()
    point_index = jnp.arange(64, dtype=jnp.int32)
    return (
        nodes_all[point_index // 16],
        nodes_all[point_index // 4 % 4],
        nodes_all[point_index % 4],
    )


def contribute(coeff_block, source_row, source_col, target_row, target_col, level_index, n_by):
    spatial = coeff_block.shape[2]
    zc_count = 2**level_index
    half_count = 8 // zc_count
    box_width = 32.0 * zc_count
    node_first, node_second, node_third = point_nodes()
    first, second, third = centers(target_row, target_col, level_index, spatial, n_by)
    side_index = jnp.arange(2, dtype=jnp.int32)
    freq_x = ((4 * side_index + source_row % 4) // zc_count).astype(jnp.float32)
    freq_y = ((4 * side_index + source_col % 4) // zc_count).astype(jnp.float32)
    freq_z = (2 * jnp.arange(half_count, dtype=jnp.int32)[:, None] + side_index[None, :]).astype(
        jnp.float32
    )
    p_first = (-256.0 + box_width * (freq_x[None, :] + 0.5 + node_first[:, None])).reshape(
        64, 1, 2, 1, 1, 1, 1, 1
    )
    p_second = (-256.0 + box_width * (freq_y[None, :] + 0.5 + node_second[:, None])).reshape(
        64, 1, 1, 2, 1, 1, 1, 1
    )
    p_third = (-256.0 + box_width * (freq_z[None] + 0.5 + node_third[:, None, None])).reshape(
        64, 1, 1, 1, 1, 1, half_count, 2
    )
    angles = phase_angle(
        first[..., None], second[..., None], third[..., None], p_first, p_second, p_third
    )
    cosines = jnp.cos(angles)
    sine_part = jnp.sin(angles)
    shaped = coeff_block.reshape(2, 64, spatial, 2, 2, zc_count, 1, half_count, 2)
    turned = jnp.stack(
        [shaped[0] * cosines - shaped[1] * sine_part, shaped[0] * sine_part + shaped[1] * cosines]
    )
    weights_stack = jnp.stack(
        [
            cube_matrix(bit_at(source_row, level_index), bit_at(source_col, level_index), 0),
            cube_matrix(bit_at(source_row, level_index), bit_at(source_col, level_index), 1),
        ],
        axis=2,
    )
    return jnp.einsum(
        "tsz,rsabcdefz->rtabcdef",
        weights_stack,
        turned,
        precision=lax.Precision.HIGHEST,
        preferred_element_type=jnp.float32,
    )


def finish(summed, target_row, target_col, level_index, n_by):
    spatial = summed.shape[2]
    zc_count = 2**level_index
    half_count = 8 // zc_count
    box_width = 64.0 * zc_count
    node_first, node_second, node_third = point_nodes()
    first, second, third = centers(target_row, target_col, level_index, spatial, n_by)
    side_index = jnp.arange(2, dtype=jnp.int32)
    freq_x = ((4 * side_index + target_row % 4) // (2 * zc_count)).astype(jnp.float32)
    freq_y = ((4 * side_index + target_col % 4) // (2 * zc_count)).astype(jnp.float32)
    freq_z = jnp.arange(half_count, dtype=jnp.int32).astype(jnp.float32)
    p_first = (-256.0 + box_width * (freq_x[None, :] + 0.5 + node_first[:, None])).reshape(
        64, 1, 2, 1, 1, 1, 1
    )
    p_second = (-256.0 + box_width * (freq_y[None, :] + 0.5 + node_second[:, None])).reshape(
        64, 1, 1, 2, 1, 1, 1
    )
    p_third = (-256.0 + box_width * (freq_z[None, :] + 0.5 + node_third[:, None])).reshape(
        64, 1, 1, 1, 1, 1, half_count
    )
    angles = phase_angle(first, second, third, p_first, p_second, p_third)
    cosines = jnp.cos(angles)
    sine_part = jnp.sin(angles)
    result = jnp.stack(
        [summed[0] * cosines + summed[1] * sine_part, summed[1] * cosines - summed[0] * sine_part]
    )
    return result.reshape(2, 64, spatial, 2, 2, 16)


def local(coefficients):
    n_bx = lax.axis_size("bx")
    n_by = lax.axis_size("by")
    top_row = n_bx.bit_length() - 2
    top_col = n_by.bit_length() - 2
    dev_row = logical_index(lax.axis_index("bx"), n_bx)
    dev_col = logical_index(lax.axis_index("by"), n_by)
    spatial = coefficients.shape[4] // 64
    coeff_block = coefficients.reshape(2, 64, spatial, 2, 2, 16)
    for level_index in range(2):
        mate_row = partner(dev_row, level_index)
        mate_col = partner(dev_col, level_index)
        row_bit = top_row - level_index
        col_bit = top_col - level_index
        outgoing = jnp.stack(
            [
                contribute(coeff_block, dev_row, dev_col, mate_row, dev_col, level_index, n_by),
                contribute(coeff_block, dev_row, dev_col, mate_row, mate_col, level_index, n_by),
            ]
        )
        arrived = swapped(outgoing, "bx", row_bit)
        kept_terms = (
            jnp.stack(
                [
                    contribute(coeff_block, dev_row, dev_col, dev_row, dev_col, level_index, n_by),
                    contribute(coeff_block, dev_row, dev_col, dev_row, mate_col, level_index, n_by),
                ]
            )
            + arrived
        )
        summed = kept_terms[0] + swapped(kept_terms[1], "by", col_bit)
        coeff_block = finish(summed, dev_row, dev_col, level_index, n_by)
    return coeff_block.reshape(1, 1, 2, 64, spatial * 64)


def solution(mesh):
    return jax.shard_map(
        local,
        mesh=mesh,
        in_specs=(P("bx", "by", None, None, None),),
        out_specs=P("bx", "by", None, None, None),
        check_vma=False,
    )
```

profile of v0, /device:TPU:1, one launch (start us, length us, event | category | flops | bytes accessed | tf_op | source)
XLA Modules:
  0.0 500.3 jit_solution(11440123779045280784)
XLA Ops:
  0.1 0.7 fusion.165
  0.7 2.6 fusion.78
  3.3 2.6 fusion.119
  7.5 0.6 multiply_add_fusion.21
  8.1 0.7 multiply_add_fusion.20
  10.1 2.1 fusion.164
  13.2 1.4 copy.28
  15.5 1.3 multiply_bitcast_fusion.3
  16.8 2.2 stack_reshape.9
  19.0 2.2 stack_reshape.8
  21.2 0.6 multiply_add_fusion.14
  21.8 0.6 multiply_add_fusion.15
  23.0 1.4 broadcast_multiply_fusion.20
  24.8 32.1 %multiply_subtract_fusion.7 = (f32[1,64,32,2,2,1,2,8,2]{1,2,8,7,6,4,3,0,5:T(8,128)S(1)}, f32[1,64,32,2,2,1,2,8,2]{1,2,8,7,6,4,3,0,5:T(8,128)S(1)}, f32[1,64,32,2...) fusion(f32[64,32,2,2,8,2]{0,1,5,4,3,2:T(8,128)S(1)} %copy.14, ...), kind=kLoop, calls=%fused_computation.79 | loop fusion | flops 10485760 | bytes 10634240 | tf_op jit(solution)/shard_map/sub | solution.py:136
  57.0 3.4 fusion.58
  60.4 3.6 fusion.59
  63.9 0.6 pad_maximum_fusion
  64.6 4.3 collective-permute-start
  69.1 3.6 fusion.60
  73.3 3.6 fusion.61
  78.1 0.7 multiply_add_fusion.12
  78.8 0.7 fusion.161
  80.1 78.0 %collective-permute-done = f32[2,2,64,32,2,2,1,2,8]{2,3,8,7,5,4,1,6,0:T(8,128)S(1)} collective-permute-done((f32[2,2,64,32,2,2,1,2,8]{2,3,8,7,5,4,1,6,0:T(8,128)S(1)}, f32[2,2,64,32,2,2,1,2,8]{2,3,8,7,5,4,1,6,0:T(8,128)S(1)}, u32[]{:S(2)}, u32[]{:S(2)}) %collective-permute-start) | collective-permute-done | bytes 2097184 | tf_op jit(solution)/shard_map/ppermute | solution.py:12
  158.1 1.4 maximum_add_fusion
  159.5 1.7 slice_bitcast_fusion.2
  161.2 1.0 copy-done
  162.1 7.7 %collective-permute-start.1 = (f32[2,64,32,2,2,1,2,8]{1,2,7,6,4,3,0,5:T(8,128)}, f32[2,64,32,2,2,1,2,8]{1,2,7,6,4,3,0,5:T(8,128)S(1)}, u32[]{:S(2)}, u32[]{:S(2)}) collective-permute-start(f32[2,64,32,2,2,1,2,8]{1,2,7,6,4,3,0,5:T(8,128)} %slice_bitcast_fusion.2), channel_id=1, source_target_pairs={{0,8},{1,9},{2,10},{3,11},{4,12},{5,13},{6,14},{7,15},{8,0},{9,1},... | collective-permute-start | bytes 3145736 | tf_op jit(solution)/shard_map/ppermute | solution.py:12
  171.5 0.8 broadcast_add_fusion.2
  172.3 0.8 broadcast_multiply_fusion.9
  173.0 1.0 broadcast_multiply_fusion.3
  174.1 56.5 %collective-permute-done.1 = f32[2,64,32,2,2,1,2,8]{1,2,7,6,4,3,0,5:T(8,128)S(1)} collective-permute-done((f32[2,64,32,2,2,1,2,8]{1,2,7,6,4,3,0,5:T(8,128)}, f32[2,64,32,2,2,1,2,8]{1,2,7,6,4,3,0,5:T(8,128)S(1)}, u32[]{:S(2)}, u32[]{:S(2)}) %collective-permute-start.1) | collective-permute-done | bytes 1048608 | tf_op jit(solution)/shard_map/ppermute | solution.py:12
  230.6 2.1 fusion.29
  232.7 4.3 multiply_add_fusion.9
  237.1 31.9 %multiply_subtract_fusion.3 = (f32[1,64,32,2,2,2,2,4,2]{1,2,8,7,6,5,4,3,0:T(8,128)S(1)}, f32[1,64,32,2,2,2,2,4,2]{1,2,8,7,6,5,4,3,0:T(8,128)S(1)}, f32[1,64,32,2...) fusion(f32[64,32,2,2,2,4,2]{0,1,6,5,4,3,2:T(8,128)S(1)} %bitcas, ...), kind=kLoop, calls=%fused_computation.59 | loop fusion | flops 10485760 | bytes 10627072 | tf_op jit(solution)/shard_map/sub | solution.py:136
  269.0 3.4 fusion.46
  272.4 3.6 fusion.49
  276.0 0.7 pad_maximum_fusion.1
  276.7 1.6 collective-permute-start.2
  278.3 3.6 fusion.52
  281.9 3.6 fusion.55
  285.4 53.5 %collective-permute-done.2 = f32[2,2,64,32,2,2,2,2,4]{2,3,8,7,6,5,4,1,0:T(8,128)S(1)} collective-permute-done((f32[2,2,64,32,2,2,2,2,4]{2,3,8,7,6,5,4,1,0:T(8,128)S(1)}, f32[2,2,64,32,2,2,2,2,4]{2,3,8,7,6,5,4,1,0:T(8,128)S(1)}, u32[]{:S(2)}, u32[]{:S(2)}) %collective-permute-start.2) | collective-permute-done | bytes 2097184 | tf_op jit(solution)/shard_map/ppermute | solution.py:12
  338.9 1.5 maximum_add_fusion.1
  340.6 60.5 %collective-permute-start.3 = (f32[2,64,32,2,2,2,2,4]{1,2,7,6,5,4,3,0:T(8,128)S(1)}, f32[2,64,32,2,2,2,2,4]{1,2,7,6,5,4,3,0:T(8,128)S(1)}, u32[]{:S(2)}, u32[]{:S(2)}) collective-permute-start(f32[2,64,32,2,2,2,2,4]{1,2,7,6,5,4,3,0:T(8,128)S(1)} %slice_bitcast_fusion), channel_id=1, source_target_pairs={{0,4},{1,5},{2,6},{3,7},{4,0},{5,1},{6,2},{7,3},{8,12},{9,13},{10,... | collective-permute-start | bytes 3145736 | tf_op jit(solution)/shard_map/ppermute | solution.py:12
  401.3 90.6 %collective-permute-done.3 = f32[2,64,32,2,2,2,2,4]{1,2,7,6,5,4,3,0:T(8,128)S(1)} collective-permute-done((f32[2,64,32,2,2,2,2,4]{1,2,7,6,5,4,3,0:T(8,128)S(1)}, f32[2,64,32,2,2,2,2,4]{1,2,7,6,5,4,3,0:T(8,128)S(1)}, u32[]{:S(2)}, u32[]{:S(2)}) %collective-permute-start.3) | collective-permute-done | bytes 1048608 | tf_op jit(solution)/shard_map/ppermute | solution.py:12
  492.4 4.3 multiply_add_fusion.8
  496.7 0.7 copy.16
  497.4 0.7 copy.15
  498.2 1.6 copy.17
  (117 shorter events, 10.5 us)
Async XLA Ops:
  3.3 75.5 %copy-start.6 = (f32[64]{0:T(128)}, f32[64]{0:T(128)S(1)}, u32[]{:S(2)}) copy-start(f32[64]{0:T(128)S(1)} %get-tuple-element.146) | copy-start | bytes 772
  6.7 15.9 %copy-start.19 = (s32[32]{0:T(128)}, s32[32]{0:T(128)S(1)}, u32[]{:S(2)}) copy-start(s32[32]{0:T(128)S(1)} %fusion.82) | copy-start | bytes 388
  22.7 2.1 copy-start.10
  22.7 34.2 %copy-start.8 = (f32[32,2]{0,1:T(2,128)}, f32[32,2]{0,1:T(2,128)S(1)}, u32[]{:S(2)}) copy-start(f32[32,2]{0,1:T(2,128)S(1)} %get-tuple-element.132) | copy-start | bytes 772
  24.7 32.2 %copy-start.2 = (f32[64,64,1]{1,0,2:T(8,128)S(1)}, f32[64,64,1]{1,0,2:T(8,128)}, u32[]{:S(2)}) copy-start(f32[64,64,1]{1,0,2:T(8,128)} %stack_reshape.9) | copy-start | bytes 49156
  24.8 32.2 %copy-start.3 = (f32[64,64,1]{1,0,2:T(8,128)S(1)}, f32[64,64,1]{1,0,2:T(8,128)}, u32[]{:S(2)}) copy-start(f32[64,64,1]{1,0,2:T(8,128)} %stack_reshape.8) | copy-start | bytes 49156
  63.9 5.0 copy-start.20
  64.6 93.6 %collective-permute-start = (f32[2,2,64,32,2,2,1,2,8]{2,3,8,7,5,4,1,6,0:T(8,128)S(1)}, f32[2,2,64,32,2,2,1,2,8]{2,3,8,7,5,4,1,6,0:T(8,128)S(1)}, u32[]{:S(2)}, u32[]{:S(2)}) collective-permute-start(f32[2,2,64,32,2,2,1,2,8]{2,3,8,7,5,4,1,6,0:T(8,128)S(1)} %pad_maximum_fusion), channel_id=1, source_target_pairs={{0,128},{16,144},{32,160},{48,176},{64,192},{80,208},{96,224},{112... | collective-permute-start | bytes 6291464 | tf_op jit(solution)/shard_map/ppermute | solution.py:12
  73.3 3.6 copy-start.18
  73.3 4.2 copy-start.17
  159.5 2.6 copy-start
  159.5 10.3 %copy-start.16 = (f32[32]{0:T(128)S(1)}, f32[32]{0:T(128)}, u32[]{:S(2)}) copy-start(f32[32]{0:T(128)} %get-tuple-element.154) | copy-start | bytes 388
  162.1 68.4 %collective-permute-start.1 = (f32[2,64,32,2,2,1,2,8]{1,2,7,6,4,3,0,5:T(8,128)}, f32[2,64,32,2,2,1,2,8]{1,2,7,6,4,3,0,5:T(8,128)S(1)}, u32[]{:S(2)}, u32[]{:S(2)}) collective-permute-start(f32[2,64,32,2,2,1,2,8]{1,2,7,6,4,3,0,5:T(8,128)} %slice_bitcast_fusion.2), channel_id=1, source_target_pairs={{0,8},{1,9},{2,10},{3,11},{4,12},{5,13},{6,14},{7,15},{8,0},{9,1},... | collective-permute-start | bytes 3145736 | tf_op jit(solution)/shard_map/ppermute | solution.py:12
  174.1 58.6 %copy-start.9 = (f32[32,2]{0,1:T(2,128)S(1)}, f32[32,2]{0,1:T(2,128)}, u32[]{:S(2)}) copy-start(f32[32,2]{0,1:T(2,128)} %copy-done.8) | copy-start | bytes 772
  232.6 4.4 copy-start.1
  232.7 4.4 copy-start.4
  232.7 4.4 copy-start.11
  232.7 4.4 copy-start.12
  232.7 4.4 copy-start.13
  276.7 62.2 %collective-permute-start.2 = (f32[2,2,64,32,2,2,2,2,4]{2,3,8,7,6,5,4,1,0:T(8,128)S(1)}, f32[2,2,64,32,2,2,2,2,4]{2,3,8,7,6,5,4,1,0:T(8,128)S(1)}, u32[]{:S(2)}, u32[]{:S(2)}) collective-permute-start(f32[2,2,64,32,2,2,2,2,4]{2,3,8,7,6,5,4,1,0:T(8,128)S(1)} %pad_maximum_fusion.1), channel_id=1, source_target_pairs={{0,64},{16,80},{32,96},{48,112},{64,0},{80,16},{96,32},{112,48},{1... | collective-permute-start | bytes 6291464 | tf_op jit(solution)/shard_map/ppermute | solution.py:12
  340.4 60.7 %copy-start.14 = (f32[64,2]{0,1:T(2,128)S(1)}, f32[64,2]{0,1:T(2,128)}, u32[]{:S(2)}) copy-start(f32[64,2]{0,1:T(2,128)} %get-tuple-element.70) | copy-start | bytes 1540
  340.4 60.7 %copy-start.15 = (f32[64,2]{0,1:T(2,128)S(1)}, f32[64,2]{0,1:T(2,128)}, u32[]{:S(2)}) copy-start(f32[64,2]{0,1:T(2,128)} %get-tuple-element.68) | copy-start | bytes 1540
  340.4 60.7 %copy-start.7 = (f32[64]{0:T(128)S(1)}, f32[64]{0:T(128)}, u32[]{:S(2)}) copy-start(f32[64]{0:T(128)} %copy-done.6) | copy-start | bytes 772
  340.4 60.8 %copy-start.5 = (f32[32,2,2]{0,2,1:T(2,128)S(1)}, f32[32,2,2]{0,2,1:T(2,128)}, u32[]{:S(2)}) copy-start(f32[32,2,2]{0,2,1:T(2,128)} %get-tuple-element.83) | copy-start | bytes 1540
  340.6 151.3 %collective-permute-start.3 = (f32[2,64,32,2,2,2,2,4]{1,2,7,6,5,4,3,0:T(8,128)S(1)}, f32[2,64,32,2,2,2,2,4]{1,2,7,6,5,4,3,0:T(8,128)S(1)}, u32[]{:S(2)}, u32[]{:S(2)}) collective-permute-start(f32[2,64,32,2,2,2,2,4]{1,2,7,6,5,4,3,0:T(8,128)S(1)} %slice_bitcast_fusion), channel_id=1, source_target_pairs={{0,4},{1,5},{2,6},{3,7},{4,0},{5,1},{6,2},{7,3},{8,12},{9,13},{10,... | collective-permute-start | bytes 3145736 | tf_op jit(solution)/shard_map/ppermute | solution.py:12
where the time goes:
time: 505 us; the launch traced here: 500 us
  waiting for transfers between devices  279 us (55%)
  other arithmetic  101 us (20%)
  starting transfers between devices  74.1 us (15%)
  matrix products  28.2 us (6%)
  local copies, waits for them, and re-layouts  16.8 us (3%)
    ppermute x4, waiting for transfers between devices, swapped(): lax.ppermute(array, axis, [(i, i ^ 1 << bit) for i in range(lax.axis_size...  279 us
    ppermute x4, starting transfers between devices, swapped(): lax.ppermute(array, axis, [(i, i ^ 1 << bit) for i in range(lax.axis_size...  74.1 us
    sub x2, other arithmetic, contribute(): shaped[0] * cosines - shaped[1] * sine_part  64.1 us
    dot_general x8, matrix products, contribute(): jnp.einsum('tsz,rsabcdefz->rtabcdef', weights_stack, turned, precision=la...  28.2 us
  transfers between devices with their start and end apart: 4, of which 4 were waited for; matrix products, arithmetic and copies ran while one was open for 5% of the time, Pallas kernels for 0%

commit v1 on v0

v1 whole, which is shorter than its diff:
```python
import functools

import jax
import jax.numpy as jnp
import ml_dtypes
import numpy as np
from jax import lax
from jax.experimental import pallas as pl
from jax.experimental.pallas import tpu as pltpu
from jax.sharding import PartitionSpec as P

MESH = pl.DeviceIdType.MESH
NODES = [float(0.5 * np.cos((2 * k + 1) * np.pi / 8)) for k in range(4)]
SIN = [
    6.283182818516952,
    -41.341421395485554,
    81.59618379063296,
    -76.58009967534186,
    41.205391074799934,
    -12.271256275754906,
]
COS = [
    0.9999999891721036,
    -19.73920453203502,
    64.93911898074299,
    -85.45016549020424,
    60.16783121892548,
    -25.968311307335807,
    6.529607525848247,
]


def child_weights(bit):
    nodes = 0.5 * np.cos((2 * np.arange(4) + 1) * np.pi / 8)
    at = (bit - 0.5) / 2 + nodes / 2
    out = np.ones((4, 4))
    for t in range(4):
        for k in range(4):
            if k != t:
                out[t] *= (at - nodes[k]) / (nodes[t] - nodes[k])
    return out


def weights():
    side = [child_weights(0), child_weights(1)]
    blocks = [
        np.kron(np.kron(side[a], side[b]), side[c]) for a in (0, 1) for b in (0, 1) for c in (0, 1)
    ]
    whole = np.concatenate(blocks, axis=1)
    high = whole.astype(ml_dtypes.bfloat16)
    low = (whole - high.astype(np.float64)).astype(ml_dtypes.bfloat16)
    return np.concatenate([high, low], axis=0)


def sincos(turns):
    turns = turns - jnp.round(turns)
    square = turns * turns
    sine = jnp.full_like(turns, SIN[-1])
    for c in SIN[-2::-1]:
        sine = sine * square + c
    cosine = jnp.full_like(turns, COS[-1])
    for c in COS[-2::-1]:
        cosine = cosine * square + c
    return cosine, sine * turns


def kernel(
    x_ref, w_ref, o_ref, xin, xe, tab0, tab1, tab2, v, wh, wl, ob, mm, lin0, lin1, kap0, dkap,
    kap2, lin2, send1, recv1, send2, recv2, own,
):
    bx, by = lax.axis_index("bx"), lax.axis_index("by")
    a, b = bx // 4, by // 4
    row, col = lax.rem(bx, 4), lax.rem(by, 4)
    a0, a1, b0, b1 = a // 2, lax.rem(a, 2), b // 2, lax.rem(b, 2)
    me = 4 * a + b

    def flipped(k):
        p0 = lax.rem(a0 + k // 8, 2)
        q0 = lax.rem(b0 + k // 4 % 2, 2)
        p1 = lax.rem(a1 + k // 2 % 2, 2)
        q1 = lax.rem(b1 + k % 2, 2)
        return p0, q0, p1, q1

    def device(k):
        p0, q0, p1, q1 = flipped(k)
        return ((2 * p0 + p1) * 4 + row, (2 * q0 + q1) * 4 + col)

    def member(k):
        p0, q0, p1, q1 = flipped(k)
        return (2 * p0 + p1) * 4 + 2 * q0 + q1

    def lanes(m):
        return pl.ds(pl.multiple_of(m * 128, 128), 128)

    def inward(k):
        return pltpu.make_async_remote_copy(
            src_ref=x_ref.at[:, :, lanes(member(k))],
            dst_ref=xin.at[me],
            send_sem=send1.at[k],
            recv_sem=recv1.at[k],
            device_id=device(k),
            device_id_type=MESH,
        )

    def outward(k):
        return pltpu.make_async_remote_copy(
            src_ref=ob.at[k],
            dst_ref=o_ref.at[:, :, lanes(me)],
            send_sem=send2.at[k],
            recv_sem=recv2.at[k],
            device_id=device(k),
            device_id_type=MESH,
        )

    barrier = pltpu.get_barrier_semaphore()
    for k in range(1, 16):
        pl.semaphore_signal(barrier, inc=1, device_id=device(k), device_id_type=MESH)
    pl.semaphore_wait(barrier, 15)
    for k in (4, 12, 5, 13, 6, 14, 7, 15, 1, 9, 3, 11, 8, 2, 10):
        inward(k).start()
    own_in = pltpu.make_async_copy(x_ref.at[:, :, lanes(me)], xin.at[me], own.at[0])
    own_in.start()
    load_weights = pltpu.make_async_copy(w_ref, mm, own.at[1])
    load_weights.start()

    group = row * 4 + col
    px, py = group // 2, lax.rem(group, 2) * 4 + a
    lane = lax.broadcasted_iota(jnp.int32, (64, 128), 1)
    point = lax.broadcasted_iota(jnp.int32, (64, 128), 0)

    def node(digit):
        out = jnp.full((64, 128), NODES[3], jnp.float32)
        for k in range(3):
            out = jnp.where(digit == k, NODES[k], out)
        return out

    zx, zy, zz = node(point // 16), node(point // 4 % 4), node(point % 4)

    def lane_bit(index, width):
        return (index // width) % 2

    def as_f32(value):
        return value.astype(jnp.float32)

    ex, ey = as_f32(lane_bit(lane, 32)), as_f32(lane_bit(lane, 16))
    u8, u4 = lane_bit(lane, 8), lane_bit(lane, 4)
    u2, u1 = lane_bit(lane, 2), lane_bit(lane, 1)
    pz = 2 * b + lane_bit(lane, 64)
    cell_z0 = 2 * pz + u8
    cell_z1 = 2 * cell_z0 + u4
    small = (8, 128)

    def spread(value):
        return jnp.full(small, value, jnp.int32).astype(jnp.float32)

    def speed(sine_x, sine_y, cosine_z):
        return 0.05 * (1.0 + 0.5 * sine_x * sine_y + 0.3 * cosine_z)

    cos_z0 = sincos(as_f32(2 * cell_z0[0:8] + 1) * (1.0 / 32))[0]
    cos_z1 = sincos(as_f32(2 * cell_z1[0:8] + 1) * (1.0 / 64))[0]
    odd_z0, odd_z1 = as_f32(2 * cell_z0 + 1), as_f32(2 * cell_z1 + 1)

    def prepare0(c, _):
        odd_x, odd_y = 2 * (2 * px + c // 2) + 1, 2 * (2 * py + lax.rem(c, 2)) + 1
        sine_x = sincos(spread(odd_x) * (1.0 / 32))[1]
        sine_y = sincos(spread(odd_y) * (1.0 / 32))[1]
        kap0[c] = speed(sine_x, sine_y, cos_z0)
        wide_x, wide_y = odd_x.astype(jnp.float32), odd_y.astype(jnp.float32)
        lin0[c] = 0.5 + wide_x * zx + wide_y * zy + odd_z0 * zz
        sign_x = (2 * (c // 2) - 1).astype(jnp.float32)
        sign_y = (2 * lax.rem(c, 2) - 1).astype(jnp.float32)
        lin1[c] = 0.5 + sign_x * zx + sign_y * zy + as_f32(2 * u4 - 1) * zz
        return 0

    lax.fori_loop(0, 4, prepare0, 0)

    def prepare1(c, _):
        first, second = c // 4, lax.rem(c, 4)
        odd_x = 2 * (2 * (2 * px + first // 2) + second // 2) + 1
        odd_y = 2 * (2 * (2 * py + lax.rem(first, 2)) + lax.rem(second, 2)) + 1
        sine_x = sincos(spread(odd_x) * (1.0 / 64))[1]
        sine_y = sincos(spread(odd_y) * (1.0 / 64))[1]
        own_speed = speed(sine_x, sine_y, cos_z1)
        kap2[c] = own_speed
        dkap[c] = own_speed - kap0[first]
        wide_x, wide_y = odd_x.astype(jnp.float32), odd_y.astype(jnp.float32)
        lin2[c] = 2.0 * (wide_x * zx + wide_y * zy + odd_z1 * zz)
        return 0

    lax.fori_loop(0, 16, prepare1, 0)

    def radius(width, fx, fy, fz):
        p1 = width * (fx + zx) + (0.5 * width - 256.0)
        p2 = width * (fy + zy) + (0.5 * width - 256.0)
        p3 = width * (fz + zz) + (0.5 * width - 256.0)
        return jnp.sqrt(p1 * p1 + p2 * p2 + p3 * p3)

    def tall(value):
        return jnp.broadcast_to(value[None], (8, 8, 128)).reshape(64, 128)

    def fill0(n, _):
        fx = 4.0 * ex + (2 * (n // 16) + n // 4 % 2).astype(jnp.float32)
        fy = 4.0 * ey + (2 * (n // 8 % 2) + n // 2 % 2).astype(jnp.float32)
        fz = as_f32(8 * u2 + 4 * u1 + 2 * u4) + (n % 2).astype(jnp.float32)
        r = radius(32.0, fx, fy, fz)
        for c in range(4):
            cosine, sine = sincos(lin0[c] + tall(kap0[c]) * r)
            tab0[c * 32 + n, 0] = cosine
            tab0[c * 32 + n, 1] = sine
        return 0

    lax.fori_loop(0, 32, fill0, 0)

    def fill1(n, _):
        fx = 2.0 * ex + (n // 4).astype(jnp.float32)
        fy = 2.0 * ey + (n // 2 % 2).astype(jnp.float32)
        fz = as_f32(4 * u2 + 2 * u1) + (n % 2).astype(jnp.float32)
        r = radius(64.0, fx, fy, fz)

        def child(first, _):
            for second in range(4):
                c = first * 4 + second
                cosine, sine = sincos(lin1[second] + tall(dkap[c]) * r)
                tab1[c * 8 + n, 0] = cosine
                tab1[c * 8 + n, 1] = sine
            return 0

        lax.fori_loop(0, 4, child, 0)
        return 0

    lax.fori_loop(0, 8, fill1, 0)

    def fill2(c, _):
        r = radius(128.0, ex, ey, as_f32(2 * u2 + u1))
        cosine, sine = sincos(lin2[c] + tall(kap2[c]) * r)
        tab2[c, 0] = cosine
        tab2[c, 1] = sine
        return 0

    lax.fori_loop(0, 16, fill2, 0)

    even = (lane // 16) * 16 + 8 * u2 + 4 * u1 + 2 * u4

    def picked(value, index):
        return jnp.take_along_axis(value, index, axis=1, mode="promise_in_bounds")

    def arrange(k):
        p0, q0, p1, q1 = flipped(k)
        m = (2 * p0 + p1) * 4 + 2 * q0 + q1
        n = (2 * p1 + q1) * 8 + (2 * p0 + q0) * 2
        for part in range(2):
            got = xin[m, part]
            xe[n, part] = picked(got, even)
            xe[n + 1, part] = picked(got, even + 1)

    def arrive(k, _):
        inward(k).wait_recv()
        arrange(k)
        return 0

    load_weights.wait()
    own_in.wait()
    arrange(0)
    lax.fori_loop(1, 16, arrive, 0)

    def turn_and_sum(turns, data):
        for n in range(8):
            cosine, sine = turns(n)
            real, imag = data(n)
            out = (real * cosine - imag * sine, real * sine + imag * cosine)
            for part in range(2):
                high = out[part].astype(jnp.bfloat16)
                at = (pl.ds(64 * n, 64), pl.ds(128 * part, 128))
                wh[at] = high
                wl[at] = (out[part] - high.astype(jnp.float32)).astype(jnp.bfloat16)
        both = jnp.dot(mm[...], wh[...], preferred_element_type=jnp.float32)
        rest = jnp.dot(mm[0:64, :], wl[...], preferred_element_type=jnp.float32)
        total = both[0:64] + (both[64:128] + rest)
        return total[:, 0:128], total[:, 128:256]

    low4 = lane - 4 * u4

    def first_child(step, _):
        k0 = 3 - step
        c0 = 2 * lax.rem(a0 + k0 // 2, 2) + lax.rem(b0 + k0 % 2, 2)

        def first_level(g, _):
            sums = turn_and_sum(
                lambda n: (tab0[c0 * 32 + g * 8 + n, 0], tab0[c0 * 32 + g * 8 + n, 1]),
                lambda n: (xe[g * 8 + n, 0], xe[g * 8 + n, 1]),
            )
            for part in range(2):
                v[2 * g, part] = picked(sums[part], low4)
                v[2 * g + 1, part] = picked(sums[part], low4 + 4)
            return 0

        lax.fori_loop(0, 4, first_level, 0)

        def second_level(step1, _):
            k1 = 3 - step1
            c1 = 2 * lax.rem(a1 + k1 // 2, 2) + lax.rem(b1 + k1 % 2, 2)
            k, c = 4 * k0 + k1, 4 * c0 + c1
            real, imag = turn_and_sum(
                lambda n: (tab1[c * 8 + n, 0], tab1[c * 8 + n, 1]),
                lambda n: (v[n, 0], v[n, 1]),
            )
            cosine, sine = tab2[c, 0], tab2[c, 1]
            ob[k, 0] = real * cosine + imag * sine
            ob[k, 1] = imag * cosine - real * sine

            @pl.when(k > 0)
            def _():
                outward(k).start()

            return 0

        lax.fori_loop(0, 4, second_level, 0)
        return 0

    lax.fori_loop(0, 4, first_child, 0)

    own_out = pltpu.make_async_copy(ob.at[0], o_ref.at[:, :, lanes(me)], own.at[2])
    own_out.start()

    def finish(k, _):
        inward(k).wait_send()
        outward(k).wait_send()
        outward(k).wait_recv()
        return 0

    lax.fori_loop(1, 16, finish, 0)
    own_out.wait()


def local(coefficients):
    shape = coefficients.shape
    block = coefficients.reshape(shape[2:])
    f32, bf16 = jnp.float32, jnp.bfloat16
    out = pl.pallas_call(
        kernel,
        out_shape=jax.ShapeDtypeStruct(block.shape, f32),
        in_specs=[pl.BlockSpec(memory_space=pl.ANY)] * 2,
        out_specs=pl.BlockSpec(memory_space=pl.ANY),
        scratch_shapes=[
            pltpu.VMEM((16, 2, 64, 128), f32),
            pltpu.VMEM((32, 2, 64, 128), f32),
            pltpu.VMEM((128, 2, 64, 128), f32),
            pltpu.VMEM((128, 2, 64, 128), f32),
            pltpu.VMEM((16, 2, 64, 128), f32),
            pltpu.VMEM((8, 2, 64, 128), f32),
            pltpu.VMEM((512, 256), bf16),
            pltpu.VMEM((512, 256), bf16),
            pltpu.VMEM((16, 2, 64, 128), f32),
            pltpu.VMEM((128, 512), bf16),
            pltpu.VMEM((4, 64, 128), f32),
            pltpu.VMEM((4, 64, 128), f32),
            pltpu.VMEM((4, 8, 128), f32),
            pltpu.VMEM((16, 8, 128), f32),
            pltpu.VMEM((16, 8, 128), f32),
            pltpu.VMEM((16, 64, 128), f32),
            pltpu.SemaphoreType.DMA((16,)),
            pltpu.SemaphoreType.DMA((16,)),
            pltpu.SemaphoreType.DMA((16,)),
            pltpu.SemaphoreType.DMA((16,)),
            pltpu.SemaphoreType.DMA((3,)),
        ],
        compiler_params=pltpu.CompilerParams(
            collective_id=0, has_side_effects=True, vmem_limit_bytes=56 * 2**20
        ),
    )(block, jnp.asarray(weights()))
    return out.reshape(shape)


def solution(mesh):
    return jax.shard_map(
        local,
        mesh=mesh,
        in_specs=(P("bx", "by", None, None, None),),
        out_specs=P("bx", "by", None, None, None),
        check_vma=False,
    )
```

time: 505 us -> 66.3 us (0.13)
  waiting for transfers between devices: 279 us -> 0 us
  other arithmetic: 101 us -> 0 us
  starting transfers between devices: 74.1 us -> 0 us
  Pallas kernels: 0 us -> 63.9 us
  matrix products: 28.2 us -> 0 us
  local copies, waits for them, and re-layouts: 16.8 us -> 2.3 us
    ppermute x4 -> x0, waiting for transfers between devices: 279 us -> none  [swapped(): lax.ppermute(array, axis, [(i, i ^ 1 << bit) for i in range(lax.axis_size...]
    ppermute x4 -> x0, starting transfers between devices: 74.1 us -> none  [swapped(): lax.ppermute(array, axis, [(i, i ^ 1 << bit) for i in range(lax.axis_size...]
    sub x3 -> x0, other arithmetic: 64.2 us -> none  [the longest x2 64.1 us: contribute(): shaped[0] * cosines - shaped[1] * sine_part]
    pallas_call x0 -> x1, Pallas kernels: none -> 63.9 us  [local(): pl.pallas_call(kernel, out_shape=jax.ShapeDtypeStruct(block.shape, f32),...]
    dot_general x8 -> x0, matrix products: 28.2 us -> none  [contribute(): jnp.einsum('tsz,rsabcdefz->rtabcdef', weights_stack, turned, precision=la...]
    add x39 -> x0, other arithmetic: 19.2 us -> none  [the longest x2 8.6 us: finish(): summed[0] * cosines + summed[1] * sine_part]
    mul x35 -> x0, other arithmetic: 8.57 us -> none  [the longest x8 2.72 us: centers(): (cell_z.astype(jnp.float32) + 0.5) * cell_size]
    another operation x5 -> x0, local copies, waits for them, and re-layouts: 6.88 us -> none  [the longest x4 5.33 us: contribute(): jnp.stack([cube_matrix(bit_at(source_row, level_index), bit_at(source_col...]
  transfers between devices with their start and end apart: 4 -> 0, of which waited for: 4 -> 0; matrix products, arithmetic and copies ran while one was open for 5% -> 0% of each run, Pallas kernels for 0% -> 0%
where the time goes in v1:
time: 66.3 us; the launch traced here: 66.2 us
  Pallas kernels  63.9 us (96%)
  local copies, waits for them, and re-layouts  2.3 us (3%)
    pallas_call x1, Pallas kernels, local(): pl.pallas_call(kernel, out_shape=jax.ShapeDtypeStruct(block.shape, f32),...  63.9 us
    unnamed x1, local copies, waits for them, and re-layouts  2.3 us

profile of v1, /device:TPU:1, one launch (start us, length us, event | category | flops | bytes accessed | tf_op | source)
XLA Modules:
  0.0 66.2 jit_solution(14935991367391310028)
XLA Ops:
  0.0 63.9 %shard_map.28 = f32[2,64,2048]{2,1,0:T(8,128)} custom-call(f32[2,64,2048]{2,1,0:T(8,128)} %bitcast.3, bf16[128,512]{1,0:T(8,128)(2,1)} %constant.2.clone.w_ref), custom_call_target="tpu_custom_call" | custom-call | tf_op jit(solution)/shard_map/pallas_call | solution.py:339
  63.9 2.3 %copy.4 = f32[1,1,2,64,2048]{4,3,2,1,0:T(8,128)} copy(f32[1,1,2,64,2048]{4,3,2,1,0:T(8,128)} %bitcast.2) | data formatting | bytes 2097152

commit v2 on v1

v2 whole, which is shorter than its diff:
```python
import math

import jax
import jax.numpy as jnp
import numpy as np
from jax import lax
from jax.experimental import pallas as pl
from jax.experimental.pallas import tpu as pltpu
from jax.sharding import PartitionSpec as P

MESH = pl.DeviceIdType.MESH
NODES = [float(0.5 * np.cos((2 * k + 1) * np.pi / 8)) for k in range(4)]
SIN = [
    6.283182818516952,
    -41.341421395485554,
    81.59618379063296,
    -76.58009967534186,
    41.205391074799934,
    -12.271256275754906,
]
COS = [
    0.9999992215592304,
    -19.738982513358035,
    64.92872650603236,
    -85.27239557297074,
    58.79403136989473,
    -21.076769129657027,
]


def weights():
    row = lax.broadcasted_iota(jnp.int32, (64, 512), 0)
    column = lax.broadcasted_iota(jnp.int32, (64, 512), 1)

    def side(bit, t, s):
        at = 0.5 * (bit.astype(jnp.float32) - 0.5) + 0.5 * chosen(s, NODES)
        out = chosen(
            t, [1.0 / math.prod(NODES[t] - z for z in NODES if z != NODES[t]) for t in range(4)]
        )
        for k in range(4):
            out = jnp.where(t == k, out, out * (at - NODES[k]))
        return out

    first = side(column // 256, row // 16, column // 16 % 4)
    second = side(column // 128 % 2, row // 4 % 4, column // 4 % 4)
    return first * second * side(column // 64 % 2, row % 4, column % 4)


def chosen(digit, values):
    out = jnp.full(digit.shape, values[3], jnp.float32)
    for k in range(3):
        out = jnp.where(digit == k, values[k], out)
    return out


def sincos(turns):
    turns = turns - jnp.round(turns)
    square = turns * turns
    sine = jnp.full_like(turns, SIN[-1])
    for c in SIN[-2::-1]:
        sine = sine * square + c
    cosine = jnp.full_like(turns, COS[-1])
    for c in COS[-2::-1]:
        cosine = cosine * square + c
    return cosine, sine * turns


def kernel(
    x_ref, o_ref, xv, xp, xin, xe, r0, r1, squares, tab0, tab1, tab2, v, wh, wl, ob, mm, lin0, lin1,
    kap0, dkap, kap2, lin2, send1, recv1, send2, recv2, loads, own,
):
    bx, by = lax.axis_index("bx"), lax.axis_index("by")
    a, b = bx // 4, by // 4
    row, col = lax.rem(bx, 4), lax.rem(by, 4)
    a0, a1, b0, b1 = a // 2, lax.rem(a, 2), b // 2, lax.rem(b, 2)
    me = 4 * a + b

    def flipped(k):
        p0 = lax.rem(a0 + k // 8, 2)
        q0 = lax.rem(b0 + k // 4 % 2, 2)
        p1 = lax.rem(a1 + k // 2 % 2, 2)
        q1 = lax.rem(b1 + k % 2, 2)
        return p0, q0, p1, q1

    def device(k):
        p0, q0, p1, q1 = flipped(k)
        return ((2 * p0 + p1) * 4 + row, (2 * q0 + q1) * 4 + col)

    def member(k):
        p0, q0, p1, q1 = flipped(k)
        return (2 * p0 + p1) * 4 + 2 * q0 + q1

    def load(k):
        at = pl.ds(pl.multiple_of(member(k) * 128, 128), 128)
        return pltpu.make_async_copy(x_ref.at[:, :, at], xv.at[k], loads.at[k])

    def inward(half, k):
        return pltpu.make_async_remote_copy(
            src_ref=xp.at[half, k],
            dst_ref=xin.at[half, k],
            send_sem=send1.at[half, k],
            recv_sem=recv1.at[half, k],
            device_id=device(k),
            device_id_type=MESH,
        )

    def outward(half, k):
        return pltpu.make_async_remote_copy(
            src_ref=ob.at[half, k],
            dst_ref=o_ref.at[me, half],
            send_sem=send2.at[half, k],
            recv_sem=recv2.at[half, k],
            device_id=device(k),
            device_id_type=MESH,
        )

    order = (4, 12, 5, 13, 6, 14, 7, 15, 1, 9, 3, 11, 8, 2, 10)
    for k in order + (0,):
        load(k).start()
    barrier = pltpu.get_barrier_semaphore()
    for k in order:
        pl.semaphore_signal(barrier, inc=1, device_id=device(k), device_id_type=MESH)
    lane = lax.broadcasted_iota(jnp.int32, (64, 128), 1)
    point = lax.broadcasted_iota(jnp.int32, (64, 128), 0)
    first_part = lane < 64

    def swapped(value):
        return pltpu.roll(value, 64, axis=1)

    def pack(k, into):
        real, imag = xv[k, 0], xv[k, 1]
        into[0, k] = jnp.where(first_part, real, swapped(imag))
        into[1, k] = jnp.where(first_part, swapped(real), imag)

    for k in order:
        load(k).wait()
        pack(k, xp)
    pl.semaphore_wait(barrier, 15)
    for half in range(2):
        for k in order:
            inward(half, k).start()
    load(0).wait()
    pack(0, xin)

    group = row * 4 + col
    px, py = group // 2, lax.rem(group, 2) * 4 + a
    zx, zy, zz = (chosen(point // w % 4, NODES) for w in (16, 4, 1))

    def lane_bit(index, width):
        return (index // width) % 2

    def as_f32(value):
        return value.astype(jnp.float32)

    ex, ey = as_f32(lane_bit(lane, 32)), as_f32(lane_bit(lane, 16))
    child, u8, u4 = lane_bit(lane, 64), lane_bit(lane, 8), lane_bit(lane, 4)
    u2, u1 = lane_bit(lane, 2), lane_bit(lane, 1)
    whole = weights()
    leading = whole.astype(jnp.bfloat16)
    mm[0:64, :] = leading
    mm[64:128, :] = (whole - leading.astype(jnp.float32)).astype(jnp.bfloat16)

    def speed(odd_x, odd_y, odd_z, scale):
        sine_x = sincos(as_f32(odd_x[0:8]) * scale)[1]
        sine_y = sincos(as_f32(odd_y[0:8]) * scale)[1]
        cosine_z = sincos(as_f32(odd_z[0:8]) * scale)[0]
        return 0.05 * (1.0 + 0.5 * sine_x * sine_y + 0.3 * cosine_z)

    def full(value):
        return jnp.full((64, 128), value, jnp.int32)

    def linear(odd_x, odd_y, odd_z):
        return as_f32(odd_x) * zx + as_f32(odd_y) * zy + as_f32(odd_z) * zz

    def prepare0(c, _):
        odd_x = 2 * (2 * px + child) + 1
        odd_y = full(2 * (2 * py + lax.rem(c, 2)) + 1)
        odd_z = 2 * (2 * (2 * b + c // 2) + u8) + 1
        kap0[c] = speed(odd_x, odd_y, odd_z, 1.0 / 32)
        lin0[c] = 0.5 + linear(odd_x, odd_y, odd_z)
        return 0

    lax.fori_loop(0, 4, prepare0, 0)

    def prepare1(c, _):
        cell_x, cell_y = 2 * px + c // 4 % 2, 2 * py + c // 2 % 2
        cell_z = 2 * (2 * b + c // 8) + u8
        parent = speed(full(2 * cell_x + 1), full(2 * cell_y + 1), 2 * cell_z + 1, 1.0 / 32)
        odd_x = full(2 * (2 * cell_x + lax.rem(c, 2)) + 1)
        odd_y, odd_z = 2 * (2 * cell_y + child) + 1, 2 * (2 * cell_z + u4) + 1
        kap2[c] = speed(odd_x, odd_y, odd_z, 1.0 / 64)
        dkap[c] = kap2[c] - parent
        lin2[c] = 2.0 * linear(odd_x, odd_y, odd_z)
        return 0

    lax.fori_loop(0, 16, prepare1, 0)
    for c in range(2):
        lin1[c] = 0.5 + linear(full(2 * c - 1), 2 * child - 1, 2 * u4 - 1)

    def square(width, at):
        p = width * at + (0.5 * width - 256.0)
        return p * p

    for n in range(4):
        squares[n] = square(32.0, 4.0 * ex + n + zx)
        squares[4 + n] = square(32.0, 4.0 * ey + n + zy)
    for n in range(2):
        squares[8 + n] = square(32.0, as_f32(8 * u2 + 4 * u1 + 2 * u4 + n) + zz)
        squares[10 + n] = square(64.0, 2.0 * ex + n + zx)
        squares[12 + n] = square(64.0, 2.0 * ey + n + zy)
        squares[14 + n] = square(64.0, as_f32(4 * u2 + 2 * u1 + n) + zz)

    def radius0(n, _):
        fx, fy = 2 * (n // 16) + n // 4 % 2, 2 * (n // 8 % 2) + n // 2 % 2
        r0[n] = jnp.sqrt(squares[fx] + squares[4 + fy] + squares[8 + n % 2])
        return 0

    def radius1(n, _):
        r1[n] = jnp.sqrt(squares[10 + n // 4] + squares[12 + n // 2 % 2] + squares[14 + n % 2])
        return 0

    lax.fori_loop(0, 32, radius0, 0)
    lax.fori_loop(0, 8, radius1, 0)
    r1[8] = jnp.sqrt(
        square(128.0, ex + zx) + square(128.0, ey + zy) + square(128.0, as_f32(2 * u2 + u1) + zz)
    )

    def tall(value):
        return jnp.broadcast_to(value[None], (8, 8, 128)).reshape(64, 128)

    def keep(table, at, turns):
        table[at, 0], table[at, 1] = sincos(turns)

    def fill(half):
        def fill0(n, _):
            for cy in range(2):
                c = half * 2 + cy
                keep(tab0, c * 32 + n, lin0[c] + tall(kap0[c]) * r0[n])
            return 0

        def fill1(step, _):
            first, n = step // 8, step % 8
            for dx in range(2):
                c = half * 8 + first * 2 + dx
                keep(tab1, c * 8 + n, lin1[dx] + tall(dkap[c]) * r1[n])
            return 0

        def fill2(step, _):
            c = half * 8 + step
            keep(tab2, c, lin2[c] + tall(kap2[c]) * r1[8])
            return 0

        lax.fori_loop(0, 32, fill0, 0)
        lax.fori_loop(0, 32, fill1, 0)
        lax.fori_loop(0, 8, fill2, 0)

    even = (lane // 16) % 4 * 16 + 8 * u2 + 4 * u1 + 2 * u4
    low4 = lane % 64 - 4 * u4

    def picked(value, index):
        return jnp.take_along_axis(value, index, axis=1, mode="promise_in_bounds")

    def arrange(half, k):
        p0, q0, p1, q1 = flipped(k)
        n = (2 * p1 + q1) * 8 + (2 * p0 + q0) * 2
        got = xin[half, k]
        for bit in range(2):
            for part in range(2):
                xe[n + bit, part] = picked(got, even + (bit + 64 * part))

    def turn_and_sum(data, table, at):
        for n in range(8):
            real, imag = data(n)
            cosine, sine = table[at + n, 0], table[at + n, 1]
            out = (real * cosine - imag * sine, real * sine + imag * cosine)
            for part in range(2):
                high = out[part].astype(jnp.bfloat16)
                where = (pl.ds(64 * n, 64), pl.ds(128 * part, 128))
                wh[where] = high
                wl[where] = (out[part] - high.astype(jnp.float32)).astype(jnp.bfloat16)
        both = jnp.dot(mm[...], wh[...], preferred_element_type=jnp.float32)
        rest = jnp.dot(mm[0:64, :], wl[...], preferred_element_type=jnp.float32)
        total = both[0:64] + (both[64:128] + rest)
        return total[:, 0:128], total[:, 128:256]

    def box(half, _):
        arrange(half, 0)

        def arrive(k, _):
            inward(half, k).wait_recv()
            arrange(half, k)
            return 0

        lax.fori_loop(1, 16, arrive, 0)

        def first_y(step, _):
            cy = lax.rem(b0 + 1 - step, 2)

            def first_level(g, _):
                sums = turn_and_sum(
                    lambda n: (xe[g * 8 + n, 0], xe[g * 8 + n, 1]),
                    tab0,
                    (half * 2 + cy) * 32 + g * 8,
                )
                for cx in range(2):
                    for bit in range(2):
                        for part in range(2):
                            v[cx * 8 + 2 * g + bit, part] = picked(
                                sums[part], low4 + (64 * cx + 4 * bit)
                            )
                return 0

            lax.fori_loop(0, 4, first_level, 0)

            def second_level(last, _):
                fx0, fx1 = 1 - last // 2, 1 - lax.rem(last, 2)
                cx, dx = lax.rem(a0 + fx0, 2), lax.rem(a1 + fx1, 2)
                c = half * 8 + cx * 4 + cy * 2 + dx
                real, imag = turn_and_sum(lambda n: (v[cx * 8 + n, 0], v[cx * 8 + n, 1]), tab1, c * 8)
                cosine, sine = tab2[c, 0], tab2[c, 1]
                into = (real * cosine + imag * sine, imag * cosine - real * sine)
                for dy in range(2):
                    k = 8 * fx0 + 4 * (1 - step) + 2 * fx1 + lax.rem(b1 + dy, 2)
                    if dy == 0:
                        ob[half, k] = jnp.where(first_part, into[0], swapped(into[1]))
                    else:
                        ob[half, k] = jnp.where(first_part, swapped(into[0]), into[1])

                    @pl.when(k > 0)
                    def _():
                        outward(half, k).start()

                return 0

            lax.fori_loop(0, 4, second_level, 0)
            return 0

        lax.fori_loop(0, 2, first_y, 0)
        return 0

    fill(0)
    fill(1)
    lax.fori_loop(0, 2, box, 0)
    own_out = [pltpu.make_async_copy(ob.at[h, 0], o_ref.at[me, h], own.at[h]) for h in range(2)]
    for copy in own_out:
        copy.start()

    def finish(k, _):
        for half in range(2):
            inward(half, k).wait_send()
            outward(half, k).wait_send()
            outward(half, k).wait_recv()
        return 0

    lax.fori_loop(1, 16, finish, 0)
    for copy in own_out:
        copy.wait()


def unpack(p_ref, o_ref, buf, sems):
    first_part = lax.broadcasted_iota(jnp.int32, (64, 128), 1) < 64
    copies = []
    for m in range(16):
        one, two = p_ref[m, 0], p_ref[m, 1]
        buf[m, 0] = jnp.where(first_part, one, pltpu.roll(two, 64, axis=1))
        buf[m, 1] = jnp.where(first_part, pltpu.roll(one, 64, axis=1), two)
        copy = pltpu.make_async_copy(buf.at[m], o_ref.at[:, :, pl.ds(128 * m, 128)], sems.at[m])
        copy.start()
        copies.append(copy)
    for copy in copies:
        copy.wait()


def local(coefficients):
    shape = coefficients.shape
    block = coefficients.reshape(shape[2:])
    f32, bf16 = jnp.float32, jnp.bfloat16
    packed = pl.pallas_call(
        kernel,
        out_shape=jax.ShapeDtypeStruct((16, 2, 64, 128), f32),
        in_specs=[pl.BlockSpec(memory_space=pl.ANY)],
        out_specs=pl.BlockSpec(memory_space=pl.ANY),
        scratch_shapes=[
            pltpu.VMEM((16, 2, 64, 128), f32),
            pltpu.VMEM((2, 16, 64, 128), f32),
            pltpu.VMEM((2, 16, 64, 128), f32),
            pltpu.VMEM((32, 2, 64, 128), f32),
            pltpu.VMEM((32, 64, 128), f32),
            pltpu.VMEM((9, 64, 128), f32),
            pltpu.VMEM((16, 64, 128), f32),
            pltpu.VMEM((128, 2, 64, 128), f32),
            pltpu.VMEM((128, 2, 64, 128), f32),
            pltpu.VMEM((16, 2, 64, 128), f32),
            pltpu.VMEM((16, 2, 64, 128), f32),
            pltpu.VMEM((512, 256), bf16),
            pltpu.VMEM((512, 256), bf16),
            pltpu.VMEM((2, 16, 64, 128), f32),
            pltpu.VMEM((128, 512), bf16),
            pltpu.VMEM((4, 64, 128), f32),
            pltpu.VMEM((2, 64, 128), f32),
            pltpu.VMEM((4, 8, 128), f32),
            pltpu.VMEM((16, 8, 128), f32),
            pltpu.VMEM((16, 8, 128), f32),
            pltpu.VMEM((16, 64, 128), f32),
            pltpu.SemaphoreType.DMA((2, 16)),
            pltpu.SemaphoreType.DMA((2, 16)),
            pltpu.SemaphoreType.DMA((2, 16)),
            pltpu.SemaphoreType.DMA((2, 16)),
            pltpu.SemaphoreType.DMA((16,)),
            pltpu.SemaphoreType.DMA((2,)),
        ],
        compiler_params=pltpu.CompilerParams(
            collective_id=0, has_side_effects=True, vmem_limit_bytes=52 * 2**20
        ),
    )(block)
    out = pl.pallas_call(
        unpack,
        out_shape=jax.ShapeDtypeStruct(block.shape, f32),
        in_specs=[pl.BlockSpec(memory_space=pltpu.VMEM)],
        out_specs=pl.BlockSpec(memory_space=pl.ANY),
        scratch_shapes=[pltpu.VMEM((16, 2, 64, 128), f32), pltpu.SemaphoreType.DMA((16,))],
        compiler_params=pltpu.CompilerParams(vmem_limit_bytes=16 * 2**20),
    )(packed)
    return out.reshape(shape)


def solution(mesh):
    return jax.shard_map(
        local,
        mesh=mesh,
        in_specs=(P("bx", "by", None, None, None),),
        out_specs=P("bx", "by", None, None, None),
        check_vma=False,
    )
```

time: 66.3 us -> 60.5 us (0.913)
  Pallas kernels: 63.9 us -> 60.4 us
  local copies, waits for them, and re-layouts: 2.3 us -> 0 us
    pallas_call x1 -> x2, Pallas kernels: 63.9 us -> 60.4 us  [the longest x1 59.2 us: local(): pl.pallas_call(kernel, out_shape=jax.ShapeDtypeStruct((16, 2, 64, 128), f...]
    unnamed x1 -> x0, local copies, waits for them, and re-layouts: 2.3 us -> none
where the time goes in v2:
time: 60.5 us; the launch traced here: 60.4 us
  Pallas kernels  60.4 us (100%)
    pallas_call x1, Pallas kernels, local(): pl.pallas_call(kernel, out_shape=jax.ShapeDtypeStruct((16, 2, 64, 128), f...  59.2 us

profile of v2, /device:TPU:1, one launch (start us, length us, event | category | flops | bytes accessed | tf_op | source)
XLA Modules:
  0.0 60.4 jit_solution(7674108278648669395)
XLA Ops:
  0.0 59.2 %shard_map.17.p_ref = f32[16,2,64,128]{3,2,1,0:T(8,128)S(1)} custom-call(f32[2,64,2048]{2,1,0:T(8,128)} %bitcast.2), custom_call_target="tpu_custom_call" | custom-call | tf_op jit(solution)/shard_map/pallas_call | solution.py:378
  59.3 1.2 %shard_map.18 = f32[2,64,2048]{2,1,0:T(8,128)} custom-call(f32[16,2,64,128]{3,2,1,0:T(8,128)S(1)} %shard_map.17.p_ref), custom_call_target="tpu_custom_call" | custom-call | tf_op jit(solution)/shard_map/pallas_call | solution.py:416

commit v3 on v2

--- a/solution.py
+++ b/solution.py
@@ -68,6 +68,7 @@
 def kernel(
     x_ref, o_ref, xv, xp, xin, xe, r0, r1, squares, tab0, tab1, tab2, v, wh, wl, ob, mm, lin0, lin1,
     kap0, dkap, kap2, lin2, send1, recv1, send2, recv2, loads, own,
+    told,
 ):
     bx, by = lax.axis_index("bx"), lax.axis_index("by")
     a, b = bx // 4, by // 4
@@ -75,23 +76,20 @@
     a0, a1, b0, b1 = a // 2, lax.rem(a, 2), b // 2, lax.rem(b, 2)
     me = 4 * a + b
 
+    def ahead(k):
+        return lax.rem(a + k // 4, 4), lax.rem(b + k % 4, 4)
+
+    def device(place):
+        return (place[0] * 4 + row, place[1] * 4 + col)
+
     def flipped(k):
-        p0 = lax.rem(a0 + k // 8, 2)
-        q0 = lax.rem(b0 + k // 4 % 2, 2)
-        p1 = lax.rem(a1 + k // 2 % 2, 2)
-        q1 = lax.rem(b1 + k % 2, 2)
-        return p0, q0, p1, q1
-
-    def device(k):
-        p0, q0, p1, q1 = flipped(k)
-        return ((2 * p0 + p1) * 4 + row, (2 * q0 + q1) * 4 + col)
-
-    def member(k):
-        p0, q0, p1, q1 = flipped(k)
-        return (2 * p0 + p1) * 4 + 2 * q0 + q1
+        x = 2 * lax.rem(a0 + k // 8, 2) + lax.rem(a1 + k // 4 % 2, 2)
+        y = 2 * lax.rem(b0 + k // 2 % 2, 2) + lax.rem(b1 + k % 2, 2)
+        return x, y
 
     def load(k):
-        at = pl.ds(pl.multiple_of(member(k) * 128, 128), 128)
+        x, y = ahead(k)
+        at = pl.ds(pl.multiple_of((4 * x + y) * 128, 128), 128)
         return pltpu.make_async_copy(x_ref.at[:, :, at], xv.at[k], loads.at[k])
 
     def inward(half, k):
@@ -100,7 +98,7 @@
             dst_ref=xin.at[half, k],
             send_sem=send1.at[half, k],
             recv_sem=recv1.at[half, k],
-            device_id=device(k),
+            device_id=device(ahead(k)),
             device_id_type=MESH,
         )
 
@@ -110,16 +108,18 @@
             dst_ref=o_ref.at[me, half],
             send_sem=send2.at[half, k],
             recv_sem=recv2.at[half, k],
-            device_id=device(k),
+            device_id=device(flipped(k)),
             device_id_type=MESH,
         )
 
-    order = (4, 12, 5, 13, 6, 14, 7, 15, 1, 9, 3, 11, 8, 2, 10)
+    along_z, along_y = (1, 2, 3), (4, 8, 12)
+    straight = along_z + along_y
+    order = straight + (6, 10, 14, 5, 9, 13, 7, 11, 15)
     for k in order + (0,):
         load(k).start()
     barrier = pltpu.get_barrier_semaphore()
-    for k in order:
-        pl.semaphore_signal(barrier, inc=1, device_id=device(k), device_id_type=MESH)
+    for k in straight:
+        pl.semaphore_signal(barrier, inc=1, device_id=device(ahead(k)), device_id_type=MESH)
     lane = lax.broadcasted_iota(jnp.int32, (64, 128), 1)
     point = lax.broadcasted_iota(jnp.int32, (64, 128), 0)
     first_part = lane < 64
@@ -135,10 +135,18 @@
     for k in order:
         load(k).wait()
         pack(k, xp)
-    pl.semaphore_wait(barrier, 15)
-    for half in range(2):
-        for k in order:
-            inward(half, k).start()
+    pl.semaphore_wait(barrier, 6)
+    for k in along_y:
+        pl.semaphore_signal(told, inc=1, device_id=device(ahead(k)), device_id_type=MESH)
+    for k in straight:
+        inward(0, k).start()
+    pl.semaphore_wait(told, 3)
+    for k in order[6:]:
+        inward(0, k).start()
+    for k in straight:
+        inward(1, k).start()
+    for k in order[6:]:
+        inward(1, k).start()
     load(0).wait()
     pack(0, xin)
 
@@ -261,8 +269,8 @@
         return jnp.take_along_axis(value, index, axis=1, mode="promise_in_bounds")
 
     def arrange(half, k):
-        p0, q0, p1, q1 = flipped(k)
-        n = (2 * p1 + q1) * 8 + (2 * p0 + q0) * 2
+        x, y = lax.rem(a + 4 - k // 4, 4), lax.rem(b + 4 - k % 4, 4)
+        n = (2 * (x % 2) + y % 2) * 8 + (2 * (x // 2) + y // 2) * 2
         got = xin[half, k]
         for bit in range(2):
             for part in range(2):
@@ -293,49 +301,43 @@
 
         lax.fori_loop(1, 16, arrive, 0)
 
-        def first_y(step, _):
-            cy = lax.rem(b0 + 1 - step, 2)
-
-            def first_level(g, _):
-                sums = turn_and_sum(
-                    lambda n: (xe[g * 8 + n, 0], xe[g * 8 + n, 1]),
-                    tab0,
-                    (half * 2 + cy) * 32 + g * 8,
-                )
-                for cx in range(2):
-                    for bit in range(2):
-                        for part in range(2):
-                            v[cx * 8 + 2 * g + bit, part] = picked(
-                                sums[part], low4 + (64 * cx + 4 * bit)
-                            )
-                return 0
-
-            lax.fori_loop(0, 4, first_level, 0)
-
-            def second_level(last, _):
-                fx0, fx1 = 1 - last // 2, 1 - lax.rem(last, 2)
-                cx, dx = lax.rem(a0 + fx0, 2), lax.rem(a1 + fx1, 2)
-                c = half * 8 + cx * 4 + cy * 2 + dx
-                real, imag = turn_and_sum(lambda n: (v[cx * 8 + n, 0], v[cx * 8 + n, 1]), tab1, c * 8)
-                cosine, sine = tab2[c, 0], tab2[c, 1]
-                into = (real * cosine + imag * sine, imag * cosine - real * sine)
-                for dy in range(2):
-                    k = 8 * fx0 + 4 * (1 - step) + 2 * fx1 + lax.rem(b1 + dy, 2)
-                    if dy == 0:
-                        ob[half, k] = jnp.where(first_part, into[0], swapped(into[1]))
-                    else:
-                        ob[half, k] = jnp.where(first_part, swapped(into[0]), into[1])
-
-                    @pl.when(k > 0)
-                    def _():
-                        outward(half, k).start()
-
-                return 0
-
-            lax.fori_loop(0, 4, second_level, 0)
-            return 0
-
-        lax.fori_loop(0, 2, first_y, 0)
+        def first_level(step, _):
+            cy, g = step // 4, step % 4
+            sums = turn_and_sum(
+                lambda n: (xe[g * 8 + n, 0], xe[g * 8 + n, 1]), tab0, (half * 2 + cy) * 32 + g * 8
+            )
+            for cx in range(2):
+                for bit in range(2):
+                    for part in range(2):
+                        v[cx * 16 + cy * 8 + 2 * g + bit, part] = picked(
+                            sums[part], low4 + (64 * cx + 4 * bit)
+                        )
+            return 0
+
+        lax.fori_loop(0, 8, first_level, 0)
+
+        def second_level(step, _):
+            flips = (11 - step) % 8
+            fx0, fx1, fy0 = flips // 2 % 2, flips // 1 % 2, flips // 4 % 2
+            cx, dx, cy = lax.rem(a0 + fx0, 2), lax.rem(a1 + fx1, 2), lax.rem(b0 + fy0, 2)
+            at, c = cx * 16 + cy * 8, half * 8 + cx * 4 + cy * 2 + dx
+            real, imag = turn_and_sum(lambda n: (v[at + n, 0], v[at + n, 1]), tab1, c * 8)
+            cosine, sine = tab2[c, 0], tab2[c, 1]
+            into = (real * cosine + imag * sine, imag * cosine - real * sine)
+            for dy in range(2):
+                k = 8 * fx0 + 4 * fx1 + 2 * fy0 + lax.rem(b1 + dy, 2)
+                if dy == 0:
+                    ob[half, k] = jnp.where(first_part, into[0], swapped(into[1]))
+                else:
+                    ob[half, k] = jnp.where(first_part, swapped(into[0]), into[1])
+
+                @pl.when(k > 0)
+                def _():
+                    outward(half, k).start()
+
+            return 0
+
+        lax.fori_loop(0, 8, second_level, 0)
         return 0
 
     fill(0)
@@ -391,7 +393,7 @@
             pltpu.VMEM((128, 2, 64, 128), f32),
             pltpu.VMEM((128, 2, 64, 128), f32),
             pltpu.VMEM((16, 2, 64, 128), f32),
-            pltpu.VMEM((16, 2, 64, 128), f32),
+            pltpu.VMEM((32, 2, 64, 128), f32),
             pltpu.VMEM((512, 256), bf16),
             pltpu.VMEM((512, 256), bf16),
             pltpu.VMEM((2, 16, 64, 128), f32),
@@ -408,6 +410,7 @@
             pltpu.SemaphoreType.DMA((2, 16)),
             pltpu.SemaphoreType.DMA((16,)),
             pltpu.SemaphoreType.DMA((2,)),
+            pltpu.SemaphoreType.REGULAR,
         ],
         compiler_params=pltpu.CompilerParams(
             collective_id=0, has_side_effects=True, vmem_limit_bytes=52 * 2**20

time: 60.5 us -> 58.3 us (0.964)
  Pallas kernels: 60.4 us -> 57.9 us
    pallas_call x1, Pallas kernels: 59.2 us -> 56.7 us  [local(): pl.pallas_call(kernel, out_shape=jax.ShapeDtypeStruct((16, 2, 64, 128), f...]
where the time goes in v3:
time: 58.3 us; the launch traced here: 57.9 us
  Pallas kernels  57.9 us (99%)
    pallas_call x1, Pallas kernels, local(): pl.pallas_call(kernel, out_shape=jax.ShapeDtypeStruct((16, 2, 64, 128), f...  56.7 us
    pallas_call x1, Pallas kernels, local(): pl.pallas_call(unpack, out_shape=jax.ShapeDtypeStruct(block.shape, f32),...  1.17 us

profile of v3, /device:TPU:1, one launch (start us, length us, event | category | flops | bytes accessed | tf_op | source)
XLA Modules:
  0.0 57.9 jit_solution(13511682776863624220)
XLA Ops:
  0.0 56.7 %shard_map.17.p_ref = f32[16,2,64,128]{3,2,1,0:T(8,128)S(1)} custom-call(f32[2,64,2048]{2,1,0:T(8,128)} %bitcast.2), custom_call_target="tpu_custom_call" | custom-call | tf_op jit(solution)/shard_map/pallas_call | solution.py:380
  56.7 1.2 %shard_map.18 = f32[2,64,2048]{2,1,0:T(8,128)} custom-call(f32[16,2,64,128]{3,2,1,0:T(8,128)S(1)} %shard_map.17.p_ref), custom_call_target="tpu_custom_call" | custom-call | tf_op jit(solution)/shard_map/pallas_call | solution.py:419

commit v4 on v3

--- a/solution.py
+++ b/solution.py
@@ -115,11 +115,11 @@
     along_z, along_y = (1, 2, 3), (4, 8, 12)
     straight = along_z + along_y
     order = straight + (6, 10, 14, 5, 9, 13, 7, 11, 15)
-    for k in order + (0,):
-        load(k).start()
     barrier = pltpu.get_barrier_semaphore()
     for k in straight:
         pl.semaphore_signal(barrier, inc=1, device_id=device(ahead(k)), device_id_type=MESH)
+    for k in order + (0,):
+        load(k).start()
     lane = lax.broadcasted_iota(jnp.int32, (64, 128), 1)
     point = lax.broadcasted_iota(jnp.int32, (64, 128), 0)
     first_part = lane < 64
@@ -132,7 +132,7 @@
         into[0, k] = jnp.where(first_part, real, swapped(imag))
         into[1, k] = jnp.where(first_part, swapped(real), imag)
 
-    for k in order:
+    for k in straight:
         load(k).wait()
         pack(k, xp)
     pl.semaphore_wait(barrier, 6)
@@ -140,6 +140,9 @@
         pl.semaphore_signal(told, inc=1, device_id=device(ahead(k)), device_id_type=MESH)
     for k in straight:
         inward(0, k).start()
+    for k in order[6:]:
+        load(k).wait()
+        pack(k, xp)
     pl.semaphore_wait(told, 3)
     for k in order[6:]:
         inward(0, k).start()
@@ -301,43 +304,48 @@
 
         lax.fori_loop(1, 16, arrive, 0)
 
-        def first_level(step, _):
-            cy, g = step // 4, step % 4
-            sums = turn_and_sum(
-                lambda n: (xe[g * 8 + n, 0], xe[g * 8 + n, 1]), tab0, (half * 2 + cy) * 32 + g * 8
-            )
-            for cx in range(2):
-                for bit in range(2):
-                    for part in range(2):
-                        v[cx * 16 + cy * 8 + 2 * g + bit, part] = picked(
-                            sums[part], low4 + (64 * cx + 4 * bit)
-                        )
+        def first_y(across, _):
+            cy = lax.rem(b0 + across, 2)
+
+            def first_level(g, _):
+                sums = turn_and_sum(
+                    lambda n: (xe[g * 8 + n, 0], xe[g * 8 + n, 1]), tab0, (half * 2 + cy) * 32 + g * 8
+                )
+                for cx in range(2):
+                    for bit in range(2):
+                        for part in range(2):
+                            v[cx * 8 + 2 * g + bit, part] = picked(
+                                sums[part], low4 + (64 * cx + 4 * bit)
+                            )
+                return 0
+
+            lax.fori_loop(0, 4, first_level, 0)
+
+            def second_level(step, _):
+                flips = (step + 1) % 4
+                fx0, fx1 = flips // 2, flips % 2
+                cx, dx = lax.rem(a0 + fx0, 2), lax.rem(a1 + fx1, 2)
+                c = half * 8 + cx * 4 + cy * 2 + dx
+                real, imag = turn_and_sum(lambda n: (v[cx * 8 + n, 0], v[cx * 8 + n, 1]), tab1, c * 8)
+                cosine, sine = tab2[c, 0], tab2[c, 1]
+                into = (real * cosine + imag * sine, imag * cosine - real * sine)
+                for dy in range(2):
+                    k = 8 * fx0 + 4 * fx1 + 2 * across + lax.rem(b1 + dy, 2)
+                    if dy == 0:
+                        ob[half, k] = jnp.where(first_part, into[0], swapped(into[1]))
+                    else:
+                        ob[half, k] = jnp.where(first_part, swapped(into[0]), into[1])
+
+                    @pl.when(k > 0)
+                    def _():
+                        outward(half, k).start()
+
+                return 0
+
+            lax.fori_loop(0, 4, second_level, 0)
             return 0
 
-        lax.fori_loop(0, 8, first_level, 0)
-
-        def second_level(step, _):
-            flips = (11 - step) % 8
-            fx0, fx1, fy0 = flips // 2 % 2, flips // 1 % 2, flips // 4 % 2
-            cx, dx, cy = lax.rem(a0 + fx0, 2), lax.rem(a1 + fx1, 2), lax.rem(b0 + fy0, 2)
-            at, c = cx * 16 + cy * 8, half * 8 + cx * 4 + cy * 2 + dx
-            real, imag = turn_and_sum(lambda n: (v[at + n, 0], v[at + n, 1]), tab1, c * 8)
-            cosine, sine = tab2[c, 0], tab2[c, 1]
-            into = (real * cosine + imag * sine, imag * cosine - real * sine)
-            for dy in range(2):
-                k = 8 * fx0 + 4 * fx1 + 2 * fy0 + lax.rem(b1 + dy, 2)
-                if dy == 0:
-                    ob[half, k] = jnp.where(first_part, into[0], swapped(into[1]))
-                else:
-                    ob[half, k] = jnp.where(first_part, swapped(into[0]), into[1])
-
-                @pl.when(k > 0)
-                def _():
-                    outward(half, k).start()
-
-            return 0
-
-        lax.fori_loop(0, 8, second_level, 0)
+        lax.fori_loop(0, 2, first_y, 0)
         return 0
 
     fill(0)
@@ -393,7 +401,7 @@
             pltpu.VMEM((128, 2, 64, 128), f32),
             pltpu.VMEM((128, 2, 64, 128), f32),
             pltpu.VMEM((16, 2, 64, 128), f32),
-            pltpu.VMEM((32, 2, 64, 128), f32),
+            pltpu.VMEM((16, 2, 64, 128), f32),
             pltpu.VMEM((512, 256), bf16),
             pltpu.VMEM((512, 256), bf16),
             pltpu.VMEM((2, 16, 64, 128), f32),

time: 58.3 us -> 57.5 us (0.986); the launches traced: 57.9 us -> 56.5 us
  Pallas kernels: 57.9 us -> 56.5 us
    pallas_call x1, Pallas kernels: 56.7 us -> 55.3 us  [local(): pl.pallas_call(kernel, out_shape=jax.ShapeDtypeStruct((16, 2, 64, 128), f...]
where the time goes in v4:
time: 57.5 us; the launch traced here: 56.5 us
  Pallas kernels  56.5 us (98%)
    pallas_call x1, Pallas kernels, local(): pl.pallas_call(kernel, out_shape=jax.ShapeDtypeStruct((16, 2, 64, 128), f...  55.3 us
    pallas_call x1, Pallas kernels, local(): pl.pallas_call(unpack, out_shape=jax.ShapeDtypeStruct(block.shape, f32),...  1.17 us

profile of v4, /device:TPU:1, one launch (start us, length us, event | category | flops | bytes accessed | tf_op | source)
XLA Modules:
  0.0 56.5 jit_solution(3086504719808787696)
XLA Ops:
  0.0 55.3 %shard_map.17.p_ref = f32[16,2,64,128]{3,2,1,0:T(8,128)S(1)} custom-call(f32[2,64,2048]{2,1,0:T(8,128)} %bitcast.2), custom_call_target="tpu_custom_call" | custom-call | tf_op jit(solution)/shard_map/pallas_call | solution.py:388
  55.3 1.2 %shard_map.18 = f32[2,64,2048]{2,1,0:T(8,128)} custom-call(f32[16,2,64,128]{3,2,1,0:T(8,128)S(1)} %shard_map.17.p_ref), custom_call_target="tpu_custom_call" | custom-call | tf_op jit(solution)/shard_map/pallas_call | solution.py:427

commit v5 on v4

--- a/solution.py
+++ b/solution.py
@@ -146,10 +146,6 @@
     pl.semaphore_wait(told, 3)
     for k in order[6:]:
         inward(0, k).start()
-    for k in straight:
-        inward(1, k).start()
-    for k in order[6:]:
-        inward(1, k).start()
     load(0).wait()
     pack(0, xin)
 
@@ -235,6 +231,11 @@
     r1[8] = jnp.sqrt(
         square(128.0, ex + zx) + square(128.0, ey + zy) + square(128.0, as_f32(2 * u2 + u1) + zz)
     )
+
+    for k in straight:
+        inward(1, k).start()
+    for k in order[6:]:
+        inward(1, k).start()
 
     def tall(value):
         return jnp.broadcast_to(value[None], (8, 8, 128)).reshape(64, 128)

time: 57.5 us -> 57.5 us (level)
  no operation moved by 1% of the time
where the time goes in v5:
time: 57.5 us; the launch traced here: 56.5 us
  Pallas kernels  56.5 us (98%)
    pallas_call x1, Pallas kernels, local(): pl.pallas_call(kernel, out_shape=jax.ShapeDtypeStruct((16, 2, 64, 128), f...  55.3 us
    pallas_call x1, Pallas kernels, local(): pl.pallas_call(unpack, out_shape=jax.ShapeDtypeStruct(block.shape, f32),...  1.17 us

profile of v5, /device:TPU:1, one launch (start us, length us, event | category | flops | bytes accessed | tf_op | source)
XLA Modules:
  0.0 56.5 jit_solution(10361267295762021604)
XLA Ops:
  0.0 55.3 %shard_map.17.p_ref = f32[16,2,64,128]{3,2,1,0:T(8,128)S(1)} custom-call(f32[2,64,2048]{2,1,0:T(8,128)} %bitcast.2), custom_call_target="tpu_custom_call" | custom-call | tf_op jit(solution)/shard_map/pallas_call | solution.py:389
  55.3 1.2 %shard_map.18 = f32[2,64,2048]{2,1,0:T(8,128)} custom-call(f32[16,2,64,128]{3,2,1,0:T(8,128)S(1)} %shard_map.17.p_ref), custom_call_target="tpu_custom_call" | custom-call | tf_op jit(solution)/shard_map/pallas_call | solution.py:428
